TPU v7x, 256 devices: a whole 4x4x8 slice. The times are simulated.
256 devices in a mesh: seg: 32 (over x_hi, z, core), rad: 8 (over x_lo, y).
Axes of the slice: x: 4 (x_hi: 2, x_lo: 2; x = x_hi * 2 + x_lo), y: 4, z: 8, core: 2. Of those that a mesh axis runs over, the one named last changes fastest.
Arguments:
- start_vector: float32 [32, 3, 8, 384, 768], P('seg', None, 'rad'), may hold values from -12 to 12
- coupling: bfloat16 [32, 3, 3, 8, 384, 768], P('seg', None, None, 'rad'), may hold values from -1.796875 to 1.796875
- advect: float32 [8], P('rad'), may hold values from 0.001 to 0.004
Outputs:
- next_basis: float32 [32, 3, 8, 384, 768], P('seg', None, 'rad')
- hessenberg: float32 [6], replicated
All inputs are finite; a program needn't handle non-finite values.
Results may differ from a plain program's by a relative error of at most 0.008.
Values may be sent and summed in bfloat16 or wider, within the bound.
A program may use at most 128 MiB of HBM per device.

v0:
```python
import math
import jax
import jax.numpy as jnp
from jax import lax
from jax.sharding import PartitionSpec as P

RADIAL_ALL = 256
WINDOW_START = 124
RADIAL_GAIN = 0.25
VISC_AXIAL = 4.0
VISC_TURN = 0.05


def with_halo(block, sides, width):
    for axis, dim in sides:
        count = lax.axis_size(axis)
        forward = [(i, i + 1) for i in range(count - 1)]
        backward = [(target, source) for source, target in forward]
        low = lax.ppermute(
            lax.slice_in_dim(block, block.shape[dim] - width, None, axis=dim), axis, forward
        )
        high = lax.ppermute(lax.slice_in_dim(block, 0, width, axis=dim), axis, backward)
        block = jnp.concatenate([low, block, high], axis=dim)
    return block


def shifted(value, axis, steps):
    count = lax.axis_size(axis)
    pairs = [(source, (source + steps) % count) for source in range(count)]
    return lax.ppermute(value, axis, pairs)


def make_tables(count):
    index = jnp.arange(count, dtype=jnp.int32)
    half_len = count // 2
    freq = jnp.where(index <= half_len, index, index - half_len)
    phase = freq[:, None] * index[None, :] % count
    angle = 2.0 * math.pi / count * phase.astype(jnp.float32)
    synth = jnp.where((index <= half_len)[:, None], jnp.cos(angle), jnp.sin(angle))
    weight = jnp.where((index == 0) | (index == half_len), 1.0 / count, 2.0 / count).astype(
        jnp.float32
    )
    analysis = weight[:, None] * synth
    return (synth.astype(jnp.bfloat16), analysis.astype(jnp.bfloat16), freq)


def make_divisor(radius_index, all_rows, freq_m, freq_k, modes_m, modes_k):
    radius = (radius_index.astype(jnp.float32) + 0.5) / all_rows
    axial = (freq_k.astype(jnp.float32) / (modes_k // 2)) ** 2
    turning = (freq_m.astype(jnp.float32) / (modes_m // 2)) ** 2
    return (
        1.0
        + VISC_AXIAL * axial[None, None, :]
        + VISC_TURN * turning[None, :, None] / (radius * radius)[:, None, None]
    )


def axial_derivative(field):
    half_len = field.shape[-1] // 2
    wavenum = jnp.arange(1, half_len, dtype=jnp.int32).astype(jnp.float32)
    zeros_col = jnp.zeros(field.shape[:-1] + (1,), jnp.float32)
    return jnp.concatenate(
        [
            zeros_col,
            wavenum * field[..., half_len + 1 :],
            zeros_col,
            -wavenum * field[..., 1:half_len],
        ],
        axis=-1,
    )


def tangent(field, couple, advect, tables, divisor):
    synth_m, anal_m, synth_k, anal_k = tables
    rounded = field.astype(jnp.bfloat16)
    padded = with_halo(rounded, (("rad", 1),), 1)
    section_one = jnp.einsum(
        "crmk,kz->crmz", rounded, synth_k, preferred_element_type=jnp.float32
    ).astype(jnp.bfloat16)
    physical = jnp.einsum("mt,crmz->crtz", synth_m, section_one, preferred_element_type=jnp.float32)
    mixed = jnp.sum(couple.astype(jnp.float32) * physical[None], axis=1).astype(jnp.bfloat16)
    section_two = jnp.einsum(
        "crtz,kz->crtk", mixed, anal_k, preferred_element_type=jnp.float32
    ).astype(jnp.bfloat16)
    spectral = jnp.einsum("mt,crtk->crmk", anal_m, section_two, preferred_element_type=jnp.float32)
    deriv = axial_derivative(field)
    widened = padded.astype(jnp.float32)
    radial = RADIAL_GAIN * (widened[:, 2:] - 2.0 * widened[:, 1:-1] + widened[:, :-2])
    return (field + spectral - advect[None, :, None, None] * deriv + radial) / divisor


def apply(vector, couple, advect, tables, divisor, received):
    field = vector
    field = tangent(field, couple, advect, tables, divisor)
    received = shifted(vector.astype(jnp.bfloat16), "seg", -1).astype(vector.dtype)
    return (field - received, received)


def projected(values, cells):
    return lax.psum(jnp.stack(values) / cells, ("seg", "rad"))


def length_sum(value, cells):
    return lax.psum(value / cells, ("seg", "rad"))


def on_device(start_vector, coupling, advect):
    vector = start_vector[0]
    couple = coupling[0]
    chans, rows_here, modes_m, modes_k = vector.shape
    all_rows = rows_here * lax.axis_size("rad")
    cells = float(lax.axis_size("seg") * chans * all_rows * modes_m * modes_k)
    synth_m, anal_m, freq_m = make_tables(modes_m)
    synth_k, anal_k, freq_k = make_tables(modes_k)
    tables = (synth_m, anal_m, synth_k, anal_k)
    radius_index = (
        WINDOW_START + lax.axis_index("rad") * rows_here + jnp.arange(rows_here, dtype=jnp.int32)
    )
    divisor = make_divisor(radius_index, RADIAL_ALL, freq_m, freq_k, modes_m, modes_k)
    total = lax.psum(jnp.sum(vector * vector) / cells, ("seg", "rad"))
    start_norm = jnp.sqrt(total)
    basis_one = vector / start_norm
    image_one, shifted_one = apply(basis_one, couple, advect, tables, divisor, None)
    upper_one = projected([jnp.sum(image_one * basis_one)], cells)[0]
    residual_one = image_one - upper_one * basis_one
    lower_one = jnp.sqrt(length_sum(jnp.sum(residual_one * residual_one), cells))
    basis_two = residual_one / lower_one
    image_two, unused = apply(basis_two, couple, advect, tables, divisor, None)
    sums_two = projected([jnp.sum(image_two * basis_one), jnp.sum(image_two * basis_two)], cells)
    upper_two = sums_two[0]
    middle_two = sums_two[1]
    residual_two = image_two - upper_two * basis_one - middle_two * basis_two
    lower_two = jnp.sqrt(length_sum(jnp.sum(residual_two * residual_two), cells))
    next_basis = residual_two / lower_two
    hessenberg = jnp.stack([start_norm, upper_one, lower_one, upper_two, middle_two, lower_two])
    return (next_basis[None], hessenberg)


def solution(mesh):
    return jax.shard_map(
        on_device,
        mesh=mesh,
        in_specs=(
            P("seg", None, "rad", None, None),
            P("seg", None, None, "rad", None, None),
            P("rad"),
        ),
        out_specs=(P("seg", None, "rad", None, None), P()),
        check_vma=False,
    )
```

profile of v0, /device:TPU:1, one launch (start us, length us, event | category | flops | bytes accessed | tf_op | source)
XLA Modules:
  0.0 573.7 jit_solution(4091980021766297315)
XLA Ops:
  0.6 3.7 multiply_reduce_fusion.5
  7.9 81.3 %psum.35 = f32[]{:T(128)} all-reduce(f32[]{:T(128)S(6)} %div.96), channel_id=1, replica_groups=mesh['seg'=32,'rad'=8] {'seg','rad'}, use_global_device_ids=true, to_apply=%region_1.2 | all-reduce | flops 1 | bytes 8 | tf_op jit(solution)/shard_map/psum | solution.py:120
  89.9 3.7 fusion.146
  100.9 14.6 %fusion.202 = bf16[3,384,768]{1,2,0:T(8,128)(2,1)} fusion(f32[1,3,1,384,768]{3,4,1,2,0:T(8,128)} %copy.5, f32[]{:T(128)} %sqrt.9, s32[768]{0:T(1024)S(1)} %add_select_fusion.2, pred[768]{0:T(1024)(128)(4,1)} %iota_compare_fusion.2), kind=kOutput, calls=%fused_computation.69.clone.2 | convolution fusion | flops 1368096768 | bytes 5312260 | tf_op jit(solution)/shard_map/crmk,kz->crmz/dot_general | solution.py:77
  115.4 7.3 %convolution_bitcast_fusion.1 = f32[3,384,768]{1,2,0:T(8,128)} fusion(s32[384]{0:T(512)S(1)} %add_select_fusion.3, pred[384]{0:T(512)(128)(4,1)} %iota_compare_fusion.5, bf16[3,384,768]{1,2,0:T(8,128)(2,1)} %fusion.202), kind=kOutput, calls=%fused_computation.51 | convolution fusion | flops 681099264 | bytes 5310336 | tf_op jit(solution)/shard_map/mt,crmz->crtz/dot_general | solution.py:80
  122.8 5.2 copy.6
  131.2 3.7 fusion
  134.9 13.6 %fusion.32.clone.5 = bf16[3,384,768]{1,2,0:T(8,128)(2,1)S(1)} fusion(bf16[3,384,768]{2,1,0:T(8,128)(2,1)S(1)} %fusion, f32[768]{0:T(1024)S(1)} %copy-done.11, s32[768]{0:T(1024)S(1)} %copy-done.9, pred[768]{0:T(1024)(128)(4,1)S(1)} %copy-done.15), kind=kOutput, calls=%fused_computation.66.clone.clone.clone.2 | convolution fusion | flops 1366917120 | bytes 3545856 | tf_op jit(solution)/shard_map/crtz,kz->crtk/dot_general | solution.py:82
  152.0 8.8 %multiply_reduce_fusion.4 = (f32[]{:T(128)}, f32[3,1,384,768]{2,3,0,1:T(8,128)}) fusion(f32[3,1,384,768]{2,3,0,1:T(8,128)S(1)} %get-tuple-element.12, bf16[3,1,384,768]{2,3,0,1:T(8,128)(2,1)} %collective-permute-done.2, f32[384,768]{0,1:T(8,128)S(1)} %broadcast_add_fusion, f32[3,3,384,768]{2,3,0,1:T(8,128)S(1)} %maximum_convert_fusion, ...), kind=kOutput, calls=%fused_computation.39 | convolution fusion | flops 695402496 | bytes 25951112 | tf_op jit(solution)/shard_map/mt,crtk->crmk/dot_general | solution.py:85
  161.5 83.7 %psum.36 = f32[1]{0:T(128)} all-reduce(f32[1]{0:T(128)} %bitcast.13), channel_id=1, replica_groups=mesh['seg'=32,'rad'=8] {'seg','rad'}, use_global_device_ids=true, to_apply=%region_4.5 | all-reduce | flops 1 | bytes 8 | tf_op jit(solution)/shard_map/psum | solution.py:100
  245.1 4.2 multiply_reduce_fusion.3
  250.1 4.1 fusion.198
  254.2 72.7 %psum.37 = f32[]{:T(128)} all-reduce(f32[]{:T(128)S(6)} %div.108), channel_id=1, replica_groups=mesh['seg'=32,'rad'=8] {'seg','rad'}, use_global_device_ids=true, to_apply=%region_6.7 | all-reduce | flops 1 | bytes 8 | tf_op jit(solution)/shard_map/psum | solution.py:104
  327.7 5.5 fusion.145
  333.2 3.8 collective-permute-start.3
  339.3 15.7 %convolution_bitcast_fusion = f32[3,384,768]{1,2,0:T(8,128)} fusion(bf16[3,1,384,768]{2,3,0,1:T(8,128)(2,1)} %get-tuple-element.9, s32[768]{0:T(1024)} %copy-done.8, pred[768]{0:T(1024)(128)(4,1)} %iota_compare_fusion.2, bf16[384,384,1]{1,0,2:T(8,128)(2,1)} %fusion.198), kind=kOutput, calls=%fused_computation.50 | convolution fusion | flops 2045804544 | bytes 5607168 | tf_op jit(solution)/shard_map/mt,crmz->crtz/dot_general | solution.py:80
  355.0 5.2 copy.7
  360.2 3.7 slice_multiply_fusion.3
  363.9 3.7 fusion.1
  367.6 13.6 %fusion.206 = bf16[3,384,768]{1,2,0:T(8,128)(2,1)S(1)} fusion(bf16[3,384,768]{2,1,0:T(8,128)(2,1)S(1)} %fusion.1, f32[768]{0:T(1024)S(1)} %copy-done.12, s32[768]{0:T(1024)S(1)} %copy-done.10, pred[768]{0:T(1024)(128)(4,1)S(1)} %copy-done.16), kind=kOutput, calls=%fused_computation.61.clone.2 | convolution fusion | flops 1366917120 | bytes 3545856 | tf_op jit(solution)/shard_map/crtz,kz->crtk/dot_general | solution.py:82
  388.8 6.3 %multiply_reduce_fusion.2 = (f32[]{:T(128)}, f32[]{:T(128)}, f32[3,1,384,768]{2,3,0,1:T(8,128)}) fusion(f32[3,1,384,768]{2,3,0,1:T(8,128)S(1)} %get-tuple-element.12, f32[3,1,384,768]{2,3,0,1:T(8,128)S(1)} %copy-done, bf16[3,1,384,768]{2,3,0,1:T(8,128)(2,1)} %collective-permute-done.5, f32[384,768]{0,1:T(8,128)S(1)} %copy-done.5, ...), kind=kLoop, calls=%fused_computation.36 | loop fusion | flops 15925246 | bytes 31256076 | tf_op jit(solution)/shard_map/reduce_sum | solution.py:129
  396.5 88.5 %psum.38 = f32[2]{0:T(128)S(1)} all-reduce(f32[2]{0:T(128)S(1)} %maximum_multiply_fusion), channel_id=1, replica_groups=mesh['seg'=32,'rad'=8] {'seg','rad'}, use_global_device_ids=true, to_apply=%region_10.11 | all-reduce | flops 2 | bytes 16 | tf_op jit(solution)/shard_map/psum | solution.py:100
  485.6 7.5 %multiply_reduce_fusion = (f32[]{:T(128)}, f32[3,1,384,768]{2,3,0,1:T(8,128)}) fusion(f32[3,1,384,768]{2,3,0,1:T(8,128)} %get-tuple-element.10, f32[]{:T(128)} %bitcast.25, f32[3,1,384,768]{2,3,0,1:T(8,128)} %get-tuple-element.8, f32[3,1,384,768]{2,3,0,1:T(8,128)S(1)} %get-tuple-element.12, f32[]{:T(128)} %bitcast.24), kind=kLoop, calls=%fused_computation.33 | loop fusion | flops 5308415 | bytes 14155788 | tf_op jit(solution)/shard_map/reduce_sum | solution.py:133
  493.7 72.6 %psum.39 = f32[]{:T(128)} all-reduce(f32[]{:T(128)S(6)} %div.113), channel_id=1, replica_groups=mesh['seg'=32,'rad'=8] {'seg','rad'}, use_global_device_ids=true, to_apply=%region_12.13 | all-reduce | flops 1 | bytes 8 | tf_op jit(solution)/shard_map/psum | solution.py:104
  (67 shorter events, 34.5 us)
Async XLA Ops:
  0.6 4.3 copy-start.1
  93.6 55.0 %collective-permute-start = (bf16[3,1,384,768]{2,3,0,1:T(8,128)(2,1)}, bf16[3,1,384,768]{2,3,0,1:T(8,128)(2,1)}, u32[]{:S(2)}, u32[]{:S(2)}) collective-permute-start(bf16[3,1,384,768]{2,3,0,1:T(8,128)(2,1)} %get-tuple-element.11), channel_id=1, source_target_pairs={{0,1},{1,2},{2,3},{3,4},{4,5},{5,6},{6,7},{8,9},{9,10},{10,11},{11... | collective-permute-start | bytes 5308424 | tf_op jit(solution)/shard_map/ppermute | solution.py:19
  96.1 52.4 %collective-permute-start.1 = (bf16[3,1,384,768]{2,3,0,1:T(8,128)(2,1)}, bf16[3,1,384,768]{2,3,0,1:T(8,128)(2,1)}, u32[]{:S(2)}, u32[]{:S(2)}) collective-permute-start(bf16[3,1,384,768]{2,3,0,1:T(8,128)(2,1)} %get-tuple-element.11), channel_id=1, source_target_pairs={{1,0},{2,1},{3,2},{4,3},{5,4},{6,5},{7,6},{9,8},{10,9},{11,10},{12... | collective-permute-start | bytes 5308424 | tf_op jit(solution)/shard_map/ppermute | solution.py:22
  97.4 54.5 %collective-permute-start.2 = (bf16[3,1,384,768]{2,3,0,1:T(8,128)(2,1)}, bf16[3,1,384,768]{2,3,0,1:T(8,128)(2,1)}, u32[]{:S(2)}, u32[]{:S(2)}) collective-permute-start(bf16[3,1,384,768]{2,3,0,1:T(8,128)(2,1)} %get-tuple-element.11), channel_id=1, source_target_pairs={{0,248},{8,0},{16,8},{24,16},{32,24},{40,32},{48,40},{56,48},{64,5... | collective-permute-start | bytes 5308424 | tf_op jit(solution)/shard_map/ppermute | solution.py:30
  98.6 16.8 %copy-start.8 = (s32[768]{0:T(1024)}, s32[768]{0:T(1024)S(1)}, u32[]{:S(2)}) copy-start(s32[768]{0:T(1024)S(1)} %add_select_fusion.2) | copy-start | bytes 9220
  128.8 23.2 %copy-start.4 = (f32[384,768]{0,1:T(8,128)}, f32[384,768]{0,1:T(8,128)S(1)}, u32[]{:S(2)}) copy-start(f32[384,768]{0,1:T(8,128)S(1)} %broadcast_add_fusion) | copy-start | bytes 3538948
  128.8 2.4 copy-start.2
  131.2 3.7 copy-start.9
  131.2 3.7 copy-start.11
  131.2 3.7 copy-start.15
  148.5 3.4 copy-start.7
  148.5 3.4 copy-start.13
  152.0 8.9 %copy-start.6 = (f32[3,1,384,1]{2,3,0,1:T(1,128)}, f32[3,1,384,1]{2,3,0,1:T(1,128)S(1)}, u32[]{:S(2)}) copy-start(f32[3,1,384,1]{2,3,0,1:T(1,128)S(1)} %concatenate.30) | copy-start | bytes 13828
  333.2 51.7 %collective-permute-start.3 = (bf16[3,1,384,768]{2,3,0,1:T(8,128)(2,1)}, bf16[3,1,384,768]{2,3,0,1:T(8,128)(2,1)}, u32[]{:S(2)}, u32[]{:S(2)}) collective-permute-start(bf16[3,1,384,768]{2,3,0,1:T(8,128)(2,1)} %get-tuple-element.9), channel_id=1, source_target_pairs={{0,1},{1,2},{2,3},{3,4},{4,5},{5,6},{6,7},{8,9},{9,10},{10,11},{11... | collective-permute-start | bytes 5308424 | tf_op jit(solution)/shard_map/ppermute | solution.py:19
  337.0 47.9 %collective-permute-start.4 = (bf16[3,1,384,768]{2,3,0,1:T(8,128)(2,1)}, bf16[3,1,384,768]{2,3,0,1:T(8,128)(2,1)}, u32[]{:S(2)}, u32[]{:S(2)}) collective-permute-start(bf16[3,1,384,768]{2,3,0,1:T(8,128)(2,1)} %get-tuple-element.9), channel_id=1, source_target_pairs={{1,0},{2,1},{3,2},{4,3},{5,4},{6,5},{7,6},{9,8},{10,9},{11,10},{12... | collective-permute-start | bytes 5308424 | tf_op jit(solution)/shard_map/ppermute | solution.py:22
  338.3 50.2 %collective-permute-start.5 = (bf16[3,1,384,768]{2,3,0,1:T(8,128)(2,1)}, bf16[3,1,384,768]{2,3,0,1:T(8,128)(2,1)}, u32[]{:S(2)}, u32[]{:S(2)}) collective-permute-start(bf16[3,1,384,768]{2,3,0,1:T(8,128)(2,1)} %get-tuple-element.9), channel_id=1, source_target_pairs={{0,248},{8,0},{16,8},{24,16},{32,24},{40,32},{48,40},{56,48},{64,5... | collective-permute-start | bytes 5308424 | tf_op jit(solution)/shard_map/ppermute | solution.py:30
  360.2 3.7 copy-start.3
  363.9 3.7 copy-start.10
  363.9 3.7 copy-start.12
  363.9 3.7 copy-start.16
  367.6 13.6 %copy-start.14 = (pred[384]{0:T(512)(128)(4,1)S(1)}, pred[384]{0:T(512)(128)(4,1)}, u32[]{:S(2)}) copy-start(pred[384]{0:T(512)(128)(4,1)} %iota_compare_fusion.5) | copy-start | bytes 1156
  384.9 3.6 copy-start.5
  384.9 3.9 copy-start
where the time goes:
time: 578 us; the launch traced here: 574 us
  blocking collectives  399 us (69%)
  matrix products  77.2 us (13%)
  other arithmetic  59.5 us (10%)
  local copies, waits for them, and re-layouts  20.5 us (4%)
  starting transfers between devices  11.1 us (2%)
  between operations  6.56 us (1%)
    psum x2, blocking collectives, projected(): return lax.psum(jnp.stack(values) / cells, ('seg', 'rad'))  172 us
    psum x2, blocking collectives, length_sum(): return lax.psum(value / cells, ('seg', 'rad'))  145 us
    psum x1, blocking collectives, on_device(): total = lax.psum(jnp.sum(vector * vector) / cells, ('seg', 'rad'))  81.3 us
    dot_general x2, matrix products, tangent(): jnp.einsum('crtz,kz->crtk', mixed, anal_k, preferred_element_type=jnp.flo...  27.2 us
    dot_general x2, matrix products, tangent(): jnp.einsum('mt,crmz->crtz', synth_m, section_one, preferred_element_type=...  23 us
    dot_general x1, matrix products, tangent(): jnp.einsum('crmk,kz->crmz', rounded, synth_k, preferred_element_type=jnp....  14.6 us
    dot_general x2, matrix products, tangent(): jnp.einsum('mt,crtk->crmk', anal_m, section_two, preferred_element_type=j...  12.4 us
  transfers between devices with their start and end apart: 6, of which 0 were waited for; matrix products, arithmetic and copies ran while one was open for 17% of the time, Pallas kernels for 0%

commit v1 on v0

--- a/solution.py
+++ b/solution.py
@@ -97,7 +97,7 @@
 
 
 def projected(values, cells):
-    return lax.psum(jnp.stack(values) / cells, ("seg", "rad"))
+    return jnp.sum(lax.all_gather(jnp.stack(values) / cells, ("seg", "rad")), axis=0)
 
 
 def length_sum(value, cells):

time: 578 us -> 1130 us (1.96)
  blocking collectives: 399 us -> 951 us
    all_gather x0 -> x1, blocking collectives: none -> 626 us  [projected(): lax.all_gather(jnp.stack(values) / cells, ('seg', 'rad'))]
    psum x2 -> x0, blocking collectives: 172 us -> none  [projected(): return lax.psum(jnp.stack(values) / cells, ('seg', 'rad'))]
    unnamed x0 -> x1, blocking collectives: none -> 83.1 us
    psum x2, blocking collectives: 145 us -> 160 us  [length_sum(): return lax.psum(value / cells, ('seg', 'rad'))]
  transfers between devices with their start and end apart: 6 -> 6, of which waited for: 0 -> 0; matrix products, arithmetic and copies ran while one was open for 17% -> 9% of each run, Pallas kernels for 0% -> 0%
where the time goes in v1:
time: 1130 us
  blocking collectives  951 us (84%)
  matrix products  77.3 us (7%)
  other arithmetic  62 us (5%)
  local copies, waits for them, and re-layouts  22.4 us (2%)
    all_gather x1, blocking collectives, projected(): lax.all_gather(jnp.stack(values) / cells, ('seg', 'rad'))  626 us
    psum x2, blocking collectives, length_sum(): return lax.psum(value / cells, ('seg', 'rad'))  160 us
    unnamed x1, blocking collectives  83.1 us
    psum x1, blocking collectives, on_device(): total = lax.psum(jnp.sum(vector * vector) / cells, ('seg', 'rad'))  81.3 us
    dot_general x2, matrix products, tangent(): jnp.einsum('crtz,kz->crtk', mixed, anal_k, preferred_element_type=jnp.flo...  27.2 us
    dot_general x2, matrix products, tangent(): jnp.einsum('mt,crmz->crtz', synth_m, section_one, preferred_element_type=...  23 us
  transfers between devices with their start and end apart: 6, of which 0 were waited for; matrix products, arithmetic and copies ran while one was open for 9% of the time, Pallas kernels for 0%

profile of v1, /device:TPU:1, one launch (start us, length us, event | category | flops | bytes accessed | tf_op | source)
XLA Modules:
  0.0 1130.0 jit_solution(12440047531318972791)
XLA Ops:
  0.6 3.7 multiply_reduce_fusion.5
  7.9 81.3 %psum.21 = f32[]{:T(128)} all-reduce(f32[]{:T(128)S(6)} %div.94), channel_id=1, replica_groups=mesh['seg'=32,'rad'=8] {'seg','rad'}, use_global_device_ids=true, to_apply=%region_1.2 | all-reduce | flops 1 | bytes 8 | tf_op jit(solution)/shard_map/psum | solution.py:120
  89.9 3.7 fusion.147
  100.9 14.6 %fusion.203 = bf16[3,384,768]{1,2,0:T(8,128)(2,1)} fusion(f32[1,3,1,384,768]{3,4,1,2,0:T(8,128)} %copy.9, f32[]{:T(128)} %sqrt.9, s32[768]{0:T(1024)S(1)} %add_select_fusion.2, pred[768]{0:T(1024)(128)(4,1)} %iota_compare_fusion.2), kind=kOutput, calls=%fused_computation.69.clone.2 | convolution fusion | flops 1368096768 | bytes 5312260 | tf_op jit(solution)/shard_map/crmk,kz->crmz/dot_general | solution.py:77
  115.5 7.3 convolution_bitcast_fusion.1
  122.8 5.2 copy.10
  131.2 3.7 fusion
  135.0 13.6 %fusion.32.clone.5 = bf16[3,384,768]{1,2,0:T(8,128)(2,1)S(1)} fusion(bf16[3,384,768]{2,1,0:T(8,128)(2,1)S(1)} %fusion, f32[768]{0:T(1024)S(1)} %copy-done.11, s32[768]{0:T(1024)S(1)} %copy-done.9, pred[768]{0:T(1024)(128)(4,1)S(1)} %copy-done.15), kind=kOutput, calls=%fused_computation.66.clone.clone.clone.2 | convolution fusion | flops 1366917120 | bytes 3545856 | tf_op jit(solution)/shard_map/crtz,kz->crtk/dot_general | solution.py:82
  152.0 8.9 multiply_reduce_fusion.4
  163.6 83.1 %all-reduce = f32[256]{0:T(256)} all-reduce(f32[256]{0:T(256)} %dynamic-update-slice), channel_id=1, replica_groups=mesh['seg'=32,'rad'=8] {'seg','rad'}, use_global_device_ids=true, to_apply=%add | all-reduce | flops 256 | bytes 2048
  247.9 4.2 multiply_reduce_fusion.3
  252.8 4.2 fusion.199
  256.9 72.7 %psum.22 = f32[]{:T(128)} all-reduce(f32[]{:T(128)S(6)} %div.105), channel_id=1, replica_groups=mesh['seg'=32,'rad'=8] {'seg','rad'}, use_global_device_ids=true, to_apply=%region_6.7 | all-reduce | flops 1 | bytes 8 | tf_op jit(solution)/shard_map/psum | solution.py:104
  330.4 5.5 fusion.146
  335.9 3.7 collective-permute-start.3
  342.0 15.7 %convolution_bitcast_fusion = f32[3,384,768]{1,2,0:T(8,128)} fusion(bf16[3,1,384,768]{2,3,0,1:T(8,128)(2,1)} %get-tuple-element.11, s32[768]{0:T(1024)} %copy-done.8, pred[768]{0:T(1024)(128)(4,1)} %iota_compare_fusion.2, bf16[384,384,1]{1,0,2:T(8,128)(2,1)} %fusion.199), kind=kOutput, calls=%fused_computation.50 | convolution fusion | flops 2045804544 | bytes 5607168 | tf_op jit(solution)/shard_map/mt,crmz->crtz/dot_general | solution.py:80
  357.7 5.2 copy.11
  362.9 3.7 slice_multiply_fusion.3
  366.6 3.7 fusion.1
  370.3 13.6 %fusion.207 = bf16[3,384,768]{1,2,0:T(8,128)(2,1)S(1)} fusion(bf16[3,384,768]{2,1,0:T(8,128)(2,1)S(1)} %fusion.1, f32[768]{0:T(1024)S(1)} %copy-done.12, s32[768]{0:T(1024)S(1)} %copy-done.10, pred[768]{0:T(1024)(128)(4,1)S(1)} %copy-done.16), kind=kOutput, calls=%fused_computation.61.clone.2 | convolution fusion | flops 1366917120 | bytes 3545856 | tf_op jit(solution)/shard_map/crtz,kz->crtk/dot_general | solution.py:82
  391.5 6.3 multiply_reduce_fusion.2
  399.2 626.4 %all-gather = f32[256,1,2]{2,1,0:T(1,128)} all-gather(f32[1,1,2]{2,1,0:T(1,128)S(1)} %fusion.112), channel_id=1, replica_groups=mesh['seg'=32,'rad'=8] {'seg','rad'}, dimensions={0}, use_global_device_ids=true | all-gather | bytes 2056 | tf_op jit(solution)/shard_map/all_gather | solution.py:100
  1027.4 7.6 multiply_reduce_fusion
  1035.5 87.2 %psum.23 = f32[]{:T(128)} all-reduce(f32[]{:T(128)S(6)} %div.110), channel_id=1, replica_groups=mesh['seg'=32,'rad'=8] {'seg','rad'}, use_global_device_ids=true, to_apply=%region_12.13 | all-reduce | flops 1 | bytes 8 | tf_op jit(solution)/shard_map/psum | solution.py:104
  (71 shorter events, 38.9 us)
Async XLA Ops:
  0.6 4.3 copy-start.1
  93.6 55.0 %collective-permute-start = (bf16[3,1,384,768]{2,3,0,1:T(8,128)(2,1)}, bf16[3,1,384,768]{2,3,0,1:T(8,128)(2,1)}, u32[]{:S(2)}, u32[]{:S(2)}) collective-permute-start(bf16[3,1,384,768]{2,3,0,1:T(8,128)(2,1)} %get-tuple-element.13), channel_id=1, source_target_pairs={{0,1},{1,2},{2,3},{3,4},{4,5},{5,6},{6,7},{8,9},{9,10},{10,11},{11... | collective-permute-start | bytes 5308424 | tf_op jit(solution)/shard_map/ppermute | solution.py:19
  96.1 52.5 %collective-permute-start.1 = (bf16[3,1,384,768]{2,3,0,1:T(8,128)(2,1)}, bf16[3,1,384,768]{2,3,0,1:T(8,128)(2,1)}, u32[]{:S(2)}, u32[]{:S(2)}) collective-permute-start(bf16[3,1,384,768]{2,3,0,1:T(8,128)(2,1)} %get-tuple-element.13), channel_id=1, source_target_pairs={{1,0},{2,1},{3,2},{4,3},{5,4},{6,5},{7,6},{9,8},{10,9},{11,10},{12... | collective-permute-start | bytes 5308424 | tf_op jit(solution)/shard_map/ppermute | solution.py:22
  97.4 54.6 %collective-permute-start.2 = (bf16[3,1,384,768]{2,3,0,1:T(8,128)(2,1)}, bf16[3,1,384,768]{2,3,0,1:T(8,128)(2,1)}, u32[]{:S(2)}, u32[]{:S(2)}) collective-permute-start(bf16[3,1,384,768]{2,3,0,1:T(8,128)(2,1)} %get-tuple-element.13), channel_id=1, source_target_pairs={{0,248},{8,0},{16,8},{24,16},{32,24},{40,32},{48,40},{56,48},{64,5... | collective-permute-start | bytes 5308424 | tf_op jit(solution)/shard_map/ppermute | solution.py:30
  98.6 16.9 %copy-start.8 = (s32[768]{0:T(1024)}, s32[768]{0:T(1024)S(1)}, u32[]{:S(2)}) copy-start(s32[768]{0:T(1024)S(1)} %add_select_fusion.2) | copy-start | bytes 9220
  128.8 23.2 %copy-start.4 = (f32[384,768]{0,1:T(8,128)}, f32[384,768]{0,1:T(8,128)S(1)}, u32[]{:S(2)}) copy-start(f32[384,768]{0,1:T(8,128)S(1)} %broadcast_add_fusion) | copy-start | bytes 3538948
  128.8 2.4 copy-start.2
  131.2 3.7 copy-start.9
  131.2 3.7 copy-start.11
  131.2 3.7 copy-start.15
  148.5 3.4 copy-start.7
  148.5 3.4 copy-start.13
  152.0 8.9 copy-start.6
  335.9 51.6 %collective-permute-start.3 = (bf16[3,1,384,768]{2,3,0,1:T(8,128)(2,1)}, bf16[3,1,384,768]{2,3,0,1:T(8,128)(2,1)}, u32[]{:S(2)}, u32[]{:S(2)}) collective-permute-start(bf16[3,1,384,768]{2,3,0,1:T(8,128)(2,1)} %get-tuple-element.11), channel_id=1, source_target_pairs={{0,1},{1,2},{2,3},{3,4},{4,5},{5,6},{6,7},{8,9},{9,10},{10,11},{11... | collective-permute-start | bytes 5308424 | tf_op jit(solution)/shard_map/ppermute | solution.py:19
  339.6 47.9 %collective-permute-start.4 = (bf16[3,1,384,768]{2,3,0,1:T(8,128)(2,1)}, bf16[3,1,384,768]{2,3,0,1:T(8,128)(2,1)}, u32[]{:S(2)}, u32[]{:S(2)}) collective-permute-start(bf16[3,1,384,768]{2,3,0,1:T(8,128)(2,1)} %get-tuple-element.11), channel_id=1, source_target_pairs={{1,0},{2,1},{3,2},{4,3},{5,4},{6,5},{7,6},{9,8},{10,9},{11,10},{12... | collective-permute-start | bytes 5308424 | tf_op jit(solution)/shard_map/ppermute | solution.py:22
  340.9 50.2 %collective-permute-start.5 = (bf16[3,1,384,768]{2,3,0,1:T(8,128)(2,1)}, bf16[3,1,384,768]{2,3,0,1:T(8,128)(2,1)}, u32[]{:S(2)}, u32[]{:S(2)}) collective-permute-start(bf16[3,1,384,768]{2,3,0,1:T(8,128)(2,1)} %get-tuple-element.11), channel_id=1, source_target_pairs={{0,248},{8,0},{16,8},{24,16},{32,24},{40,32},{48,40},{56,48},{64,5... | collective-permute-start | bytes 5308424 | tf_op jit(solution)/shard_map/ppermute | solution.py:30
  362.9 3.7 copy-start.3
  366.6 3.7 copy-start.10
  366.6 3.7 copy-start.12
  366.6 3.7 copy-start.16
  370.3 13.6 %copy-start.14 = (pred[384]{0:T(512)(128)(4,1)S(1)}, pred[384]{0:T(512)(128)(4,1)}, u32[]{:S(2)}) copy-start(pred[384]{0:T(512)(128)(4,1)} %iota_compare_fusion.5) | copy-start | bytes 1156
  387.5 3.6 copy-start.5
  387.6 3.9 copy-start
